TPU v7x, 32 devices: a whole 2x2x4 slice. The times are simulated.
32 devices in a mesh: batch: 1, blk: 4 (over x, core), box: 8 (over z, y).
Axes of the slice: x: 2, y: 2, z: 4, core: 2. Of those that a mesh axis runs over, the one named last changes fastest.
Arguments:
- surface_points: float32 [3, 4096], P(None, ('blk', 'box')), may hold values from -4 to 4
- angle_ids: int32 [128], P('batch'), may hold values from 0 to 16383
- near_mask: int32 [32, 8], P(('blk', 'box')), may hold values 0 or 1
- skeleton: int32 [32, 32], P(('blk', 'box')), may hold values from 0 to 127, as said below
- box_inverse_parts: float32 [32, 2, 128, 128], P(('blk', 'box')), may hold values from -0.375 to 0.375
- near_coupling: float32 [32, 8, 2, 32, 128], P(('blk', 'box')), may hold values from -0.25 to 0.25
- top_inverse: float32 [4, 2, 256, 256], P('blk', None, 'box'), may hold values from -0.25 to 0.25
Outputs:
- scattered: float32 [2, 128, 4096], P(None, ('batch', 'box'), 'blk')
Inputs may be any that keep to these rules, and one draw needn't show every extreme that they name: `skeleton`: each row holds 32 distinct row numbers of a box.
All inputs are finite; a program needn't handle non-finite values. No bound on the sum of `near_mask` on one device may be relied on, other than what follows from the above.
Results may differ from a plain program's by a relative error of at most 0.0003.
Values sent between devices are 32-bit elements; how exact they have to be, the bound alone decides.
No kernel may reach another device: no remote copies, remote signals or barrier semaphores. Data moves between devices by JAX's collectives and lax.ppermute only.
A program may use at most 64 MiB of HBM per device.

v0:
```python
import functools

import jax
import jax.numpy as jnp
import numpy as np
from jax import lax
from jax.experimental import pallas as pl
from jax.experimental.pallas import tpu as pltpu
from jax.sharding import PartitionSpec as P

SWEEP = 16384
WAVENUMBER = 24.0
F32 = jnp.float32
BF16 = jnp.bfloat16
VMEM = pl.BlockSpec(memory_space=pltpu.VMEM)
NN = (((1,), (0,)), ((), ()))
NT = (((1,), (1,)), ((), ()))
TN = (((0,), (0,)), ((), ()))

HALF_PI_1 = float(np.float32(201.0 / 128.0))
HALF_PI_2 = float(np.float32(np.round((np.pi / 2 - HALF_PI_1) * 2.0**22) / 2.0**22))
HALF_PI_3 = float(np.float32(np.pi / 2 - HALF_PI_1 - HALF_PI_2))


def cat(parts, axis):
    return jnp.concatenate(parts, axis=axis)


def dot(a, b, form=NN):
    return lax.dot_general(a, b, form, preferred_element_type=F32)


def split(x):
    high = x.astype(BF16)
    return high, (x - high.astype(F32)).astype(BF16)


def dot3(a, b, form=NN):
    return dot(a[0], b[0], form) + (dot(a[0], b[1], form) + dot(a[1], b[0], form))


def both(pair, function):
    return function(pair[0]), function(pair[1])


def sin_cos_small(r):
    s = r * r
    sin = r + r * s * (-1.6666654611e-1 + s * (8.3321608736e-3 - s * 1.9515295891e-4))
    cos = 1.0 - 0.5 * s + s * s * (4.166664568298827e-2 + s * (-1.388731625493765e-3 + s * 2.443315711809948e-5))
    return sin, cos


def by_quadrant(quadrant, sin, cos):
    odd = (quadrant & 1) == 1
    out_sin = jnp.where(odd, cos, sin)
    out_cos = jnp.where(odd, sin, cos)
    out_sin = jnp.where((quadrant & 2) == 2, -out_sin, out_sin)
    out_cos = jnp.where(((quadrant + 1) & 2) == 2, -out_cos, out_cos)
    return out_sin, out_cos


def one_hot(skeleton, width):
    rows = lax.broadcasted_iota(jnp.int32, (width, skeleton.shape[1]), 0)
    return jnp.where(rows == skeleton, 1.0, 0.0).astype(BF16)


def rows_form(re, im):
    return cat([cat([re, -im], 1), cat([im, re], 1)], 0)


def columns_form(re, im):
    return cat([cat([re, im], 1), cat([-im, re], 1)], 0)


def field_kernel(points_in, angles_in, skeleton_in, inverse_in, top_in, u_out, static_out, high_out, low_out,
                 points, angles, skeleton, inverse, top, sems):
    copies = [
        pltpu.make_async_copy(source, target, sems.at[k])
        for k, (source, target) in enumerate((
            (angles_in, angles), (points_in, points), (skeleton_in, skeleton), (inverse_in, inverse), (top_in, top),
        ))
    ]
    for copy in copies:
        copy.start()
    count = angles.shape[1]
    width = points.shape[1]
    rank = skeleton.shape[1]
    copies[0].wait()
    ids = angles[...]
    quadrant = (ids + SWEEP // 8) >> (SWEEP.bit_length() - 3)
    rest = ids - quadrant * (SWEEP // 4)
    sin, cos = by_quadrant(quadrant, *sin_cos_small(rest.astype(F32) * (2.0 * np.pi / SWEEP)))
    pick = lax.broadcasted_iota(jnp.int32, (8, count), 0) == 0
    columns = jnp.where(pick, cos, sin).T
    cos_column = columns[:, 0:1]
    sin_column = columns[:, 1:2]
    copies[1].wait()
    x = points[0:1, :] * WAVENUMBER
    yz = points[1:2, :] * (0.6 * WAVENUMBER) + points[2:3, :] * (0.8 * WAVENUMBER)
    phase = x * cos_column + yz * sin_column
    turns = jnp.round(phase * (2.0 / np.pi))
    r = ((phase - turns * HALF_PI_1) - turns * HALF_PI_2) - turns * HALF_PI_3
    field_sin, field_cos = by_quadrant(turns.astype(jnp.int32), *sin_cos_small(r))
    field = split(cat([field_cos, field_sin], 1))
    high_out[...] = field[0]
    low_out[...] = field[1]
    copies[2].wait()
    picker = one_hot(skeleton[...], width)
    copies[3].wait()
    parts = split(cat([inverse[0, 0], inverse[0, 1]], 1))
    rows = dot(picker, cat(parts, 1), TN)
    rows_high = rows[:, : 2 * width]
    rows_low = rows[:, 2 * width :]
    whole = rows_high + rows_low
    form = both((rows_high, rows_low), lambda v: rows_form(v[:, :width], v[:, width:]).astype(BF16))
    u_out[...] = dot3(form, field, NT)
    depth = top.shape[3]
    copies[4].wait()
    for part in range(2):
        at = slice(part * rank, (part + 1) * rank)
        static_out[at, :depth] = top[0, part]
        static_out[at, depth:] = whole[:, part * width : (part + 1) * width]


def coupling_kernel(high, low, skeleton, mask, inverse, coupling, base_out, high_out, low_out):
    width = inverse.shape[2]
    sides = coupling.shape[1]
    rank = coupling.shape[3]
    depth = sides * rank
    field = (high[...], low[...])
    re = split(inverse[0, 0])
    im = split(inverse[0, 1])
    row_matrix = (rows_form(re[0], im[0]), rows_form(re[1], im[1]))
    column_matrix = (columns_form(re[0], im[0]), columns_form(re[1], im[1]))
    picker = one_hot(skeleton[...], width)
    zero = jnp.zeros_like(picker)
    picker2 = cat([cat([picker, zero], 1), cat([zero, picker], 1)], 0)
    z = split(dot3(field, row_matrix, NT))
    u = dot(z[0], picker2) + dot(z[1], picker2)
    near = []
    for side in range(sides):
        weight = mask[0, side].astype(F32)
        near.append(cat([coupling[0, side, 0] * weight, coupling[0, side, 1] * weight], 1))
    near = split(cat(near, 0))
    base_out[:, : 2 * width] = dot3(z, column_matrix)
    base_out[:, 2 * width :] = u
    applied = split(dot3(near, column_matrix))
    for k, out in enumerate((high_out, low_out)):
        chosen = dot(near[k], picker2).astype(BF16)
        for matrix, at, part in ((applied[k], 0, width), (chosen, 2 * width, rank)):
            out[:depth, at : at + 2 * part] = matrix
            out[depth:, at : at + part] = -matrix[:, part:]
            out[depth:, at + part : at + 2 * part] = matrix[:, :part]


def join_kernel(left, u, right, mine, came, row_out, pair_out):
    row_out[0] = left[...]
    row_out[1] = u[...]
    row_out[2] = right[...]
    pair_out[0] = mine[...]
    pair_out[1] = came[...]


def message_kernel(up, middle, down, base, high, low, out):
    boxes = out.shape[0]
    count = base.shape[0]
    width = out.shape[2]
    rank = up.shape[1] // 2
    share = count // boxes
    half = share // 2
    order = (up[0], up[1], up[2], middle[0], middle[2], down[0], down[1], down[2])
    stacked = cat([v[:rank] for v in order] + [v[rank:] for v in order], 0)
    near = split(stacked.T)
    w = base[...] - dot3(near, (high[...], low[...]))
    for box in range(boxes):
        at = box * share
        out[box, :share] = w[at : at + share, :width]
        out[box, share : 2 * share] = w[at : at + share, width : 2 * width]
        t = w[at : at + share, 2 * width :]
        out[box, 2 * share : 2 * share + half] = cat([t[:half], t[half:]], 1)


def top_kernel(offsets, message, *refs):
    static_in, out = refs[:-1], refs[-1]
    boxes = message.shape[0]
    width = message.shape[2]
    share = out.shape[1]
    half = share // 2
    rank = static_in[0].shape[1] // 2
    depth = boxes * rank
    me = lax.axis_index("box")
    t_re = []
    t_im = []
    for box in range(boxes):
        packed = message[box, 2 * share : 2 * share + half]
        t = cat([packed[:, : 2 * rank], packed[:, 2 * rank :]], 0)
        t_re.append(t[:, :rank])
        t_im.append(t[:, rank:])
    t = split(cat(t_re + t_im, 1))
    static = [v[k] for v in static_in for k in range(v.shape[0])]
    top = []
    for v in static:
        top.append(rows_form(v[:rank, :depth], v[rank:, :depth]))
    y = dot3(t, split(cat(top, 0)), NT)
    for k, v in enumerate(static):
        box = k if offsets is None else me ^ offsets[k]
        local = split(columns_form(v[:rank, depth:], v[rank:, depth:]))
        part = split(y[:, k * 2 * rank : (k + 1) * 2 * rank])
        x = dot3(part, local)
        at = pl.ds(pl.multiple_of(box * width, width), width)
        out[0, :, at] = message[box, :share] + x[:, :width]
        out[1, :, at] = message[box, share : 2 * share] + x[:, width:]


def call(kernel, outs, *arrays, smem=(), hbm=(), scratch=()):
    spaces = {i: pl.BlockSpec(memory_space=pltpu.SMEM) for i in smem}
    spaces.update({i: pl.BlockSpec(memory_space=pltpu.HBM) for i in hbm})
    return pl.pallas_call(
        kernel,
        out_shape=[jax.ShapeDtypeStruct(shape, dtype) for shape, dtype in outs],
        in_specs=[spaces.get(i, VMEM) for i in range(len(arrays))],
        out_specs=[VMEM] * len(outs),
        scratch_shapes=scratch,
        compiler_params=pltpu.CompilerParams(vmem_limit_bytes=40 * 1024 * 1024),
    )(*arrays)


def shifted(value, axis, step):
    count = lax.axis_size(axis)
    return lax.ppermute(value, axis, [(i, (i + step) % count) for i in range(count)])


def swapped(value, axis, bit):
    return lax.ppermute(value, axis, [(i, i ^ bit) for i in range(lax.axis_size(axis))])


def on_device(surface_points, angle_ids, near_mask, skeleton, box_inverse_parts, near_coupling, top_inverse):
    boxes = lax.axis_size("box")
    width = box_inverse_parts.shape[2]
    count = angle_ids.shape[0]
    rank = skeleton.shape[1]
    sides = near_mask.shape[1]
    depth = top_inverse.shape[3]
    share = count // boxes
    arrays = (surface_points, angle_ids.reshape(1, count), skeleton, box_inverse_parts, top_inverse)
    arrays = [pltpu.with_memory_space_constraint(v, pltpu.HBM) for v in arrays]
    u, static, high, low = call(
        field_kernel,
        [
            ((2 * rank, count), F32),
            ((2 * rank, depth + width), F32),
            ((count, 2 * width), BF16),
            ((count, 2 * width), BF16),
        ],
        *arrays,
        hbm=range(len(arrays)),
        scratch=[pltpu.VMEM(v.shape, v.dtype) for v in arrays] + [pltpu.SemaphoreType.DMA((len(arrays),))],
    )
    left = shifted(u, "box", 1)
    right = shifted(u, "box", -1)
    if boxes == 8:
        came = swapped(static, "box", 4)
        row, pair = call(
            join_kernel, [((3,) + u.shape, F32), ((2,) + static.shape, F32)], left, u, right, static, came
        )
        over_two = swapped(pair, "box", 2)
        over_one = swapped(pair, "box", 1)
        over_three = swapped(over_one[:1], "box", 2)
        over_seven = swapped(over_two[1:], "box", 1)
        static = (pair, over_two, over_one, over_three, over_seven)
        offsets = (0, 4, 2, 6, 1, 5, 3, 7)
    else:
        row = jnp.stack([left, u, right])
        static = (lax.all_gather(static, "box"),)
        offsets = None
    up = shifted(row, "blk", 1)
    down = shifted(row, "blk", -1)
    base, matrix_high, matrix_low = call(
        coupling_kernel,
        [
            ((count, 2 * width + 2 * rank), F32),
            ((2 * sides * rank, 2 * width + 2 * rank), BF16),
            ((2 * sides * rank, 2 * width + 2 * rank), BF16),
        ],
        high, low, skeleton, near_mask, box_inverse_parts, near_coupling, smem=(3,),
    )
    rows = 2 * share + -(-share // 16) * 8
    (message,) = call(
        message_kernel, [((boxes, rows, width), F32)],
        up, row, down, base, matrix_high, matrix_low,
    )
    message = lax.all_to_all(message, "box", split_axis=0, concat_axis=0, tiled=True)
    (out,) = call(
        functools.partial(top_kernel, offsets), [((2, share, boxes * width), F32)], message, *static
    )
    return out


def solution(mesh):
    return jax.shard_map(
        on_device,
        mesh=mesh,
        in_specs=(
            P(None, ("blk", "box")),
            P("batch"),
            P(("blk", "box"), None),
            P(("blk", "box"), None),
            P(("blk", "box"), None, None, None),
            P(("blk", "box"), None, None, None, None),
            P("blk", None, "box", None),
        ),
        out_specs=P(None, ("batch", "box"), "blk"),
        check_vma=False,
    )
```

profile of v0, /device:TPU:0, one launch (start us, length us, event | category | flops | bytes accessed | tf_op | source)
XLA Modules:
  0.0 34.5 jit_solution(435035267203797135)
XLA Ops:
  0.0 1.4 %shard_map.73 = (f32[64,128]{1,0:T(8,128)S(1)}, f32[64,384]{1,0:T(8,128)S(1)}, bf16[128,256]{1,0:T(8,128)(2,1)S(1)}, bf16[128,256]{1,0:T(8,128)(2,1)S(1)}) custom-call(f32[3,128]{1,0:T(4,128)} %points_in.1, s32[1,128]{1,0:T(1,128)} %bitcast.1, s32[1,32]{1,0:T(1,128)} %skeleton.1, f32[1,2,128,128]{3,2,1,0:T(8,128)} %inverse.1, f32[1,2,32,256]{3,2,1,0:T(8,128)} %top_in.1), custom_call_target="tpu_custom_call" | custom-call | tf_op jit(solution)/shard_map/pallas_call | solution.py:218
  1.4 4.1 %collective-permute-start.2 = (f32[64,384]{1,0:T(8,128)S(1)}, f32[64,384]{1,0:T(8,128)S(1)}, u32[]{:S(2)}, u32[]{:S(2)}) collective-permute-start(f32[64,384]{1,0:T(8,128)S(1)} %get-tuple-element.15.mine), channel_id=1, source_target_pairs={{0,4},{1,5},{2,6},{3,7},{4,0},{5,1},{6,2},{7,3},{8,12},{9,13},{10,... | collective-permute-start | bytes 294920 | tf_op jit(solution)/shard_map/ppermute | solution.py:234
  5.5 1.5 %collective-permute-start = (f32[64,128]{1,0:T(8,128)S(1)}, f32[64,128]{1,0:T(8,128)S(1)}, u32[]{:S(2)}, u32[]{:S(2)}) collective-permute-start(f32[64,128]{1,0:T(8,128)S(1)} %get-tuple-element.14.u), channel_id=1, source_target_pairs={{0,1},{1,2},{2,3},{3,4},{4,5},{5,6},{6,7},{7,0},{8,9},{9,10},{10,1... | collective-permute-start | bytes 98312 | tf_op jit(solution)/shard_map/ppermute | solution.py:230
  7.0 3.2 %collective-permute-start.1 = (f32[64,128]{1,0:T(8,128)S(1)}, f32[64,128]{1,0:T(8,128)S(1)}, u32[]{:S(2)}, u32[]{:S(2)}) collective-permute-start(f32[64,128]{1,0:T(8,128)S(1)} %get-tuple-element.14.u), channel_id=1, source_target_pairs={{0,7},{1,0},{2,1},{3,2},{4,3},{5,4},{6,5},{7,6},{8,15},{9,8},{10,9... | collective-permute-start | bytes 98312 | tf_op jit(solution)/shard_map/ppermute | solution.py:230
  10.2 1.9 %collective-permute-done.left = f32[64,128]{1,0:T(8,128)S(1)} collective-permute-done((f32[64,128]{1,0:T(8,128)S(1)}, f32[64,128]{1,0:T(8,128)S(1)}, u32[]{:S(2)}, u32[]{:S(2)}) %collective-permute-start) | collective-permute-done | bytes 32800 | tf_op jit(solution)/shard_map/ppermute | solution.py:230
  12.1 0.0 collective-permute-done.1.right
  12.1 0.0 collective-permute-done.2.came
  12.2 0.1 collective-permute-start.3
  12.2 1.7 %collective-permute-start.4 = (f32[3,64,128]{2,1,0:T(8,128)S(1)}, f32[3,64,128]{2,1,0:T(8,128)S(1)}, u32[]{:S(2)}, u32[]{:S(2)}) collective-permute-start(f32[3,64,128]{2,1,0:T(8,128)S(1)} %get-tuple-element.16.middle), channel_id=1, source_target_pairs={{0,24},{8,0},{16,8},{24,16},{1,25},{9,1},{17,9},{25,17},{2,26},{10... | collective-permute-start | bytes 294920 | tf_op jit(solution)/shard_map/ppermute | solution.py:230
  14.0 1.2 %collective-permute-start.6 = (f32[2,64,384]{2,1,0:T(8,128)S(1)}, f32[2,64,384]{2,1,0:T(8,128)S(1)}, u32[]{:S(2)}, u32[]{:S(2)}) collective-permute-start(f32[2,64,384]{2,1,0:T(8,128)S(1)} %get-tuple-element.22.refs_0_), channel_id=1, source_target_pairs={{0,1},{1,0},{2,3},{3,2},{4,5},{5,4},{6,7},{7,6},{8,9},{9,8},{10,11... | collective-permute-start | bytes 589832 | tf_op jit(solution)/shard_map/ppermute | solution.py:234
  15.2 0.1 collective-permute-start.5
  15.3 0.6 %copy-done.2 = s32[1,32]{1,0:T(1,128)S(1)} copy-done((s32[1,32]{1,0:T(1,128)S(1)}, s32[1,32]{1,0:T(1,128)}, u32[]{:S(2)}) %copy-start.2) | copy-done | bytes 152
  15.9 0.0 copy-done.3
  15.9 1.4 %shard_map.75 = (f32[128,320]{1,0:T(8,128)S(1)}, bf16[512,320]{1,0:T(8,128)(2,1)S(1)}, bf16[512,320]{1,0:T(8,128)(2,1)S(1)}) custom-call(bf16[128,256]{1,0:T(8,128)(2,1)S(1)} %get-tuple-element.17.high, bf16[128,256]{1,0:T(8,128)(2,1)S(1)} %get-tuple-element.18.low, s32[1,32]{1,0:T(1,128)S(1)} %copy-done.2, s32[1,8]{1,0:T(1,128)S(1)} %copy-done.3, ...), custom_call_target="tpu_custom_call" | custom-call | tf_op jit(solution)/shard_map/pallas_call | solution.py:218
  17.3 0.0 collective-permute-done.3.up
  17.3 0.0 collective-permute-done.4.down
  17.3 1.2 %shard_map.76 = f32[8,40,128]{2,1,0:T(8,128)} custom-call(f32[3,64,128]{2,1,0:T(8,128)S(1)} %collective-permute-done.3.up, f32[3,64,128]{2,1,0:T(8,128)S(1)} %get-tuple-element.16.middle, f32[3,64,128]{2,1,0:T(8,128)S(1)} %collective-permute-done.4.down, f32[128,320]{1,0:T(8,128)S(1)} %get-tuple-element.19.base, ...), custom_call_target="tpu_custom_call" | custom-call | tf_op jit(solution)/shard_map/pallas_call | solution.py:218
  18.5 5.8 %all-to-all-start = ((f32[8,40,128]{2,1,0:T(8,128)}), f32[8,40,128]{2,1,0:T(8,128)S(1)}, u32[]{:S(2)}, u32[]{:S(2)}) async-start(f32[8,40,128]{2,1,0:T(8,128)} %shard_map.76), calls=%async_computation | async-start | bytes 327680 | tf_op jit(solution)/shard_map/all_to_all | solution.py:292
  24.4 2.1 %collective-permute-start.7 = (f32[1,64,384]{2,1,0:T(8,128)S(1)}, f32[1,64,384]{2,1,0:T(8,128)S(1)}, u32[]{:S(2)}, u32[]{:S(2)}) collective-permute-start(f32[1,64,384]{2,1,0:T(8,128)S(1)} %slice.8), channel_id=1, source_target_pairs={{0,2},{1,3},{2,0},{3,1},{4,6},{5,7},{6,4},{7,5},{8,10},{9,11},{10,... | collective-permute-start | bytes 294920 | tf_op jit(solution)/shard_map/ppermute | solution.py:234
  26.4 1.5 %collective-permute-start.8 = (f32[1,64,384]{2,1,0:T(8,128)S(1)}, f32[1,64,384]{2,1,0:T(8,128)S(1)}, u32[]{:S(2)}, u32[]{:S(2)}) collective-permute-start(f32[1,64,384]{2,1,0:T(8,128)S(1)} %slice.9), channel_id=1, source_target_pairs={{0,1},{1,0},{2,3},{3,2},{4,5},{5,4},{6,7},{7,6},{8,9},{9,8},{10,11... | collective-permute-start | bytes 294920 | tf_op jit(solution)/shard_map/ppermute | solution.py:234
  28.0 4.6 %collective-permute-done.7.refs_3_ = f32[1,64,384]{2,1,0:T(8,128)S(1)} collective-permute-done((f32[1,64,384]{2,1,0:T(8,128)S(1)}, f32[1,64,384]{2,1,0:T(8,128)S(1)}, u32[]{:S(2)}, u32[]{:S(2)}) %collective-permute-start.7) | collective-permute-done | bytes 98336 | tf_op jit(solution)/shard_map/ppermute | solution.py:234
  32.6 0.0 collective-permute-done.8.refs_4_
  32.6 0.4 %all-to-all-done.message = f32[8,40,128]{2,1,0:T(8,128)S(1)} async-done(((f32[8,40,128]{2,1,0:T(8,128)}), f32[8,40,128]{2,1,0:T(8,128)S(1)}, u32[]{:S(2)}, u32[]{:S(2)}) %all-to-all-start) | async-done | bytes 163872 | tf_op jit(solution)/shard_map/all_to_all | solution.py:292
  33.0 1.5 %shard_map.77 = f32[2,16,1024]{2,1,0:T(8,128)} custom-call(f32[8,40,128]{2,1,0:T(8,128)S(1)} %all-to-all-done.message, f32[2,64,384]{2,1,0:T(8,128)S(1)} %get-tuple-element.22.refs_0_, f32[2,64,384]{2,1,0:T(8,128)S(1)} %collective-permute-done.5.refs_1_, f32[2,64,384]{2,1,0:T(8,128)S(1)} %collective-permute-done.6.refs_2_, ...), custom_call_target="tpu_custom_call" | custom-call | tf_op jit(solution)/shard_map/pallas_call | solution.py:218
  (11 shorter events, 0.1 us)
Async XLA Ops:
  0.0 15.3 %copy-start.1 = (f32[1,8,2,32,128]{4,3,2,1,0:T(8,128)S(1)}, f32[1,8,2,32,128]{4,3,2,1,0:T(8,128)}, u32[]{:S(2)}) copy-start(f32[1,8,2,32,128]{4,3,2,1,0:T(8,128)} %coupling.1) | copy-start | bytes 786436
  1.4 10.7 %collective-permute-start.2 = (f32[64,384]{1,0:T(8,128)S(1)}, f32[64,384]{1,0:T(8,128)S(1)}, u32[]{:S(2)}, u32[]{:S(2)}) collective-permute-start(f32[64,384]{1,0:T(8,128)S(1)} %get-tuple-element.15.mine), channel_id=1, source_target_pairs={{0,4},{1,5},{2,6},{3,7},{4,0},{5,1},{6,2},{7,3},{8,12},{9,13},{10,... | collective-permute-start | bytes 294920 | tf_op jit(solution)/shard_map/ppermute | solution.py:234
  5.5 9.8 %copy-start = (f32[1,2,128,128]{3,2,1,0:T(8,128)S(1)}, f32[1,2,128,128]{3,2,1,0:T(8,128)}, u32[]{:S(2)}) copy-start(f32[1,2,128,128]{3,2,1,0:T(8,128)} %inverse.1) | copy-start | bytes 393220
  5.5 6.6 %collective-permute-start = (f32[64,128]{1,0:T(8,128)S(1)}, f32[64,128]{1,0:T(8,128)S(1)}, u32[]{:S(2)}, u32[]{:S(2)}) collective-permute-start(f32[64,128]{1,0:T(8,128)S(1)} %get-tuple-element.14.u), channel_id=1, source_target_pairs={{0,1},{1,2},{2,3},{3,4},{4,5},{5,6},{6,7},{7,0},{8,9},{9,10},{10,1... | collective-permute-start | bytes 98312 | tf_op jit(solution)/shard_map/ppermute | solution.py:230
  7.0 5.1 %collective-permute-start.1 = (f32[64,128]{1,0:T(8,128)S(1)}, f32[64,128]{1,0:T(8,128)S(1)}, u32[]{:S(2)}, u32[]{:S(2)}) collective-permute-start(f32[64,128]{1,0:T(8,128)S(1)} %get-tuple-element.14.u), channel_id=1, source_target_pairs={{0,7},{1,0},{2,1},{3,2},{4,3},{5,4},{6,5},{7,6},{8,15},{9,8},{10,9... | collective-permute-start | bytes 98312 | tf_op jit(solution)/shard_map/ppermute | solution.py:230
  12.2 5.1 %collective-permute-start.3 = (f32[3,64,128]{2,1,0:T(8,128)S(1)}, f32[3,64,128]{2,1,0:T(8,128)S(1)}, u32[]{:S(2)}, u32[]{:S(2)}) collective-permute-start(f32[3,64,128]{2,1,0:T(8,128)S(1)} %get-tuple-element.16.middle), channel_id=1, source_target_pairs={{0,8},{8,16},{16,24},{24,0},{1,9},{9,17},{17,25},{25,1},{2,10},{10... | collective-permute-start | bytes 294920 | tf_op jit(solution)/shard_map/ppermute | solution.py:230
  12.2 5.1 %collective-permute-start.4 = (f32[3,64,128]{2,1,0:T(8,128)S(1)}, f32[3,64,128]{2,1,0:T(8,128)S(1)}, u32[]{:S(2)}, u32[]{:S(2)}) collective-permute-start(f32[3,64,128]{2,1,0:T(8,128)S(1)} %get-tuple-element.16.middle), channel_id=1, source_target_pairs={{0,24},{8,0},{16,8},{24,16},{1,25},{9,1},{17,9},{25,17},{2,26},{10... | collective-permute-start | bytes 294920 | tf_op jit(solution)/shard_map/ppermute | solution.py:230
  14.0 10.4 %collective-permute-start.6 = (f32[2,64,384]{2,1,0:T(8,128)S(1)}, f32[2,64,384]{2,1,0:T(8,128)S(1)}, u32[]{:S(2)}, u32[]{:S(2)}) collective-permute-start(f32[2,64,384]{2,1,0:T(8,128)S(1)} %get-tuple-element.22.refs_0_), channel_id=1, source_target_pairs={{0,1},{1,0},{2,3},{3,2},{4,5},{5,4},{6,7},{7,6},{8,9},{9,8},{10,11... | collective-permute-start | bytes 589832 | tf_op jit(solution)/shard_map/ppermute | solution.py:234
  15.2 11.2 %collective-permute-start.5 = (f32[2,64,384]{2,1,0:T(8,128)S(1)}, f32[2,64,384]{2,1,0:T(8,128)S(1)}, u32[]{:S(2)}, u32[]{:S(2)}) collective-permute-start(f32[2,64,384]{2,1,0:T(8,128)S(1)} %get-tuple-element.22.refs_0_), channel_id=1, source_target_pairs={{0,2},{1,3},{2,0},{3,1},{4,6},{5,7},{6,4},{7,5},{8,10},{9,11},{10,... | collective-permute-start | bytes 589832 | tf_op jit(solution)/shard_map/ppermute | solution.py:234
  15.3 0.7 %copy-start.2 = (s32[1,32]{1,0:T(1,128)S(1)}, s32[1,32]{1,0:T(1,128)}, u32[]{:S(2)}) copy-start(s32[1,32]{1,0:T(1,128)} %skeleton.1) | copy-start | bytes 388
  15.3 0.7 %copy-start.3 = (s32[1,8]{1,0:T(1,128)S(1)}, s32[1,8]{1,0:T(1,128)}, u32[]{:S(2)}) copy-start(s32[1,8]{1,0:T(1,128)} %mask.1) | copy-start | bytes 100
  18.5 14.5 %all-to-all-start = ((f32[8,40,128]{2,1,0:T(8,128)}), f32[8,40,128]{2,1,0:T(8,128)S(1)}, u32[]{:S(2)}, u32[]{:S(2)}) async-start(f32[8,40,128]{2,1,0:T(8,128)} %shard_map.76), calls=%async_computation | async-start | bytes 327680 | tf_op jit(solution)/shard_map/all_to_all | solution.py:292
  24.4 8.2 %collective-permute-start.7 = (f32[1,64,384]{2,1,0:T(8,128)S(1)}, f32[1,64,384]{2,1,0:T(8,128)S(1)}, u32[]{:S(2)}, u32[]{:S(2)}) collective-permute-start(f32[1,64,384]{2,1,0:T(8,128)S(1)} %slice.8), channel_id=1, source_target_pairs={{0,2},{1,3},{2,0},{3,1},{4,6},{5,7},{6,4},{7,5},{8,10},{9,11},{10,... | collective-permute-start | bytes 294920 | tf_op jit(solution)/shard_map/ppermute | solution.py:234
  26.4 6.1 %collective-permute-start.8 = (f32[1,64,384]{2,1,0:T(8,128)S(1)}, f32[1,64,384]{2,1,0:T(8,128)S(1)}, u32[]{:S(2)}, u32[]{:S(2)}) collective-permute-start(f32[1,64,384]{2,1,0:T(8,128)S(1)} %slice.9), channel_id=1, source_target_pairs={{0,1},{1,0},{2,3},{3,2},{4,5},{5,4},{6,7},{7,6},{8,9},{9,8},{10,11... | collective-permute-start | bytes 294920 | tf_op jit(solution)/shard_map/ppermute | solution.py:234
where the time goes:
time: 34.8 us; the launch traced here: 34.5 us
  starting transfers between devices  21.3 us (61%)
  waiting for transfers between devices  6.92 us (20%)
  Pallas kernels  5.5 us (16%)
  local copies, waits for them, and re-layouts  0.68 us (2%)
    ppermute x5, starting transfers between devices, swapped(): lax.ppermute(value, axis, [(i, i ^ bit) for i in range(lax.axis_size(axis...  9 us
    ppermute x4, starting transfers between devices, shifted(): lax.ppermute(value, axis, [(i, (i + step) % count) for i in range(count)])  6.51 us
    all_to_all x1, starting transfers between devices, on_device(): lax.all_to_all(message, 'box', split_axis=0, concat_axis=0, tiled=True)  5.83 us
    pallas_call x5, Pallas kernels, call(): pl.pallas_call(kernel, out_shape=[jax.ShapeDtypeStruct(shape, dtype) for...  5.5 us
    ppermute x5, waiting for transfers between devices, swapped(): lax.ppermute(value, axis, [(i, i ^ bit) for i in range(lax.axis_size(axis...  4.62 us
    ppermute x4, waiting for transfers between devices, shifted(): lax.ppermute(value, axis, [(i, (i + step) % count) for i in range(count)])  1.9 us
  transfers between devices with their start and end apart: 10, of which 3 were waited for; matrix products, arithmetic and copies ran while one was open for 0% of the time, Pallas kernels for 7%

commit v1 on v0

--- a/solution.py
+++ b/solution.py
@@ -122,7 +122,18 @@
         static_out[at, depth:] = whole[:, part * width : (part + 1) * width]
 
 
-def coupling_kernel(high, low, skeleton, mask, inverse, coupling, base_out, high_out, low_out):
+def coupling_kernel(high, low, skeleton_in, mask_in, inverse_in, coupling_in, base_out, high_out, low_out,
+                    skeleton, mask, inverse, coupling, sems):
+    copies = [
+        pltpu.make_async_copy(source, target, sems.at[k])
+        for k, (source, target) in enumerate((
+            (skeleton_in, skeleton), (mask_in, mask), (inverse_in, inverse), (coupling_in, coupling),
+        ))
+    ]
+    for copy in copies:
+        copy.start()
+    for copy in copies:
+        copy.wait()
     width = inverse.shape[2]
     sides = coupling.shape[1]
     rank = coupling.shape[3]
@@ -139,7 +150,7 @@
     u = dot(z[0], picker2) + dot(z[1], picker2)
     near = []
     for side in range(sides):
-        weight = mask[0, side].astype(F32)
+        weight = mask[:, side : side + 1].astype(F32)
         near.append(cat([coupling[0, side, 0] * weight, coupling[0, side, 1] * weight], 1))
     near = split(cat(near, 0))
     base_out[:, : 2 * width] = dot3(z, column_matrix)
@@ -153,12 +164,12 @@
             out[depth:, at + part : at + 2 * part] = matrix[:, :part]
 
 
-def join_kernel(left, u, right, mine, came, row_out, pair_out):
+def join_kernel(base, left, u, right, two, four, row_out, pair_out):
     row_out[0] = left[...]
     row_out[1] = u[...]
     row_out[2] = right[...]
-    pair_out[0] = mine[...]
-    pair_out[1] = came[...]
+    pair_out[0] = two[...]
+    pair_out[1] = four[...]
 
 
 def message_kernel(up, middle, down, base, high, low, out):
@@ -186,7 +197,7 @@
     width = message.shape[2]
     share = out.shape[1]
     half = share // 2
-    rank = static_in[0].shape[1] // 2
+    rank = static_in[0].shape[-2] // 2
     depth = boxes * rank
     me = lax.axis_index("box")
     t_re = []
@@ -197,7 +208,7 @@
         t_re.append(t[:, :rank])
         t_im.append(t[:, rank:])
     t = split(cat(t_re + t_im, 1))
-    static = [v[k] for v in static_in for k in range(v.shape[0])]
+    static = [block for v in static_in for block in ([v[k] for k in range(v.shape[0])] if len(v.shape) == 3 else [v[...]])]
     top = []
     for v in static:
         top.append(rows_form(v[:rank, :depth], v[rank:, :depth]))
@@ -212,9 +223,13 @@
         out[1, :, at] = message[box, share : 2 * share] + x[:, width:]
 
 
-def call(kernel, outs, *arrays, smem=(), hbm=(), scratch=()):
-    spaces = {i: pl.BlockSpec(memory_space=pltpu.SMEM) for i in smem}
-    spaces.update({i: pl.BlockSpec(memory_space=pltpu.HBM) for i in hbm})
+def call(kernel, outs, *arrays, hbm=(), copied=()):
+    spaces = {i: pl.BlockSpec(memory_space=pl.ANY) for i in hbm}
+    spaces.update({i: pl.BlockSpec(memory_space=pltpu.HBM) for i in copied})
+    scratch = [pltpu.VMEM(arrays[i].shape, arrays[i].dtype) for i in copied]
+    if scratch:
+        scratch.append(pltpu.SemaphoreType.DMA((len(scratch),)))
+    arrays = [pltpu.with_memory_space_constraint(v, pltpu.HBM) if i in copied else v for i, v in enumerate(arrays)]
     return pl.pallas_call(
         kernel,
         out_shape=[jax.ShapeDtypeStruct(shape, dtype) for shape, dtype in outs],
@@ -243,7 +258,6 @@
     depth = top_inverse.shape[3]
     share = count // boxes
     arrays = (surface_points, angle_ids.reshape(1, count), skeleton, box_inverse_parts, top_inverse)
-    arrays = [pltpu.with_memory_space_constraint(v, pltpu.HBM) for v in arrays]
     u, static, high, low = call(
         field_kernel,
         [
@@ -253,28 +267,8 @@
             ((count, 2 * width), BF16),
         ],
         *arrays,
-        hbm=range(len(arrays)),
-        scratch=[pltpu.VMEM(v.shape, v.dtype) for v in arrays] + [pltpu.SemaphoreType.DMA((len(arrays),))],
-    )
-    left = shifted(u, "box", 1)
-    right = shifted(u, "box", -1)
-    if boxes == 8:
-        came = swapped(static, "box", 4)
-        row, pair = call(
-            join_kernel, [((3,) + u.shape, F32), ((2,) + static.shape, F32)], left, u, right, static, came
-        )
-        over_two = swapped(pair, "box", 2)
-        over_one = swapped(pair, "box", 1)
-        over_three = swapped(over_one[:1], "box", 2)
-        over_seven = swapped(over_two[1:], "box", 1)
-        static = (pair, over_two, over_one, over_three, over_seven)
-        offsets = (0, 4, 2, 6, 1, 5, 3, 7)
-    else:
-        row = jnp.stack([left, u, right])
-        static = (lax.all_gather(static, "box"),)
-        offsets = None
-    up = shifted(row, "blk", 1)
-    down = shifted(row, "blk", -1)
+        copied=range(len(arrays)),
+    )
     base, matrix_high, matrix_low = call(
         coupling_kernel,
         [
@@ -282,8 +276,26 @@
             ((2 * sides * rank, 2 * width + 2 * rank), BF16),
             ((2 * sides * rank, 2 * width + 2 * rank), BF16),
         ],
-        high, low, skeleton, near_mask, box_inverse_parts, near_coupling, smem=(3,),
-    )
+        high, low, skeleton, near_mask, box_inverse_parts, near_coupling, copied=range(2, 6),
+    )
+    left = shifted(u, "box", 1)
+    right = shifted(u, "box", -1)
+    if boxes == 8:
+        four = swapped(static, "box", 4)
+        two = swapped(static, "box", 2)
+        one = swapped(static, "box", 1)
+        row, pair = call(
+            join_kernel, [((3,) + u.shape, F32), ((2,) + static.shape, F32)],
+            base, left, u, right, two, four, hbm=(0,),
+        )
+        static = (static, four, two, one, swapped(pair, "box", 1), swapped(four, "box", 2), swapped(four, "box", 3))
+        offsets = (0, 4, 2, 1, 3, 5, 6, 7)
+    else:
+        row = jnp.stack([left, u, right])
+        static = (lax.all_gather(static, "box"),)
+        offsets = None
+    up = shifted(row, "blk", 1)
+    down = shifted(row, "blk", -1)
     rows = 2 * share + -(-share // 16) * 8
     (message,) = call(
         message_kernel, [((boxes, rows, width), F32)],

time: 34.8 us -> 40.5 us (1.16)
  waiting for transfers between devices: 6.92 us -> 10.5 us
  starting transfers between devices: 21.3 us -> 23.6 us
  local copies, waits for them, and re-layouts: 0.68 us -> 0 us
  Pallas kernels: 5.5 us -> 6.01 us
    ppermute x5 -> x6, waiting for transfers between devices: 4.62 us -> 8.16 us  [swapped(): lax.ppermute(value, axis, [(i, i ^ bit) for i in range(lax.axis_size(axis...]
    ppermute x5 -> x6, starting transfers between devices: 9 us -> 11.2 us  [swapped(): lax.ppermute(value, axis, [(i, i ^ bit) for i in range(lax.axis_size(axis...]
    unnamed x8 -> x0, local copies, waits for them, and re-layouts: 0.67 us -> none
    pallas_call x5, Pallas kernels: 5.5 us -> 6.01 us  [call(): pl.pallas_call(kernel, out_shape=[jax.ShapeDtypeStruct(shape, dtype) for...]
    ppermute x4, waiting for transfers between devices: 1.9 us -> 2.37 us  [shifted(): lax.ppermute(value, axis, [(i, (i + step) % count) for i in range(count)])]
  transfers between devices with their start and end apart: 10 -> 11, of which waited for: 3 -> 3; matrix products, arithmetic and copies ran while one was open for 0% -> 0% of each run, Pallas kernels for 7% -> 5%
where the time goes in v1:
time: 40.5 us; the launch traced here: 40.2 us
  starting transfers between devices  23.6 us (58%)
  waiting for transfers between devices  10.5 us (26%)
  Pallas kernels  6.01 us (15%)
    ppermute x6, starting transfers between devices, swapped(): lax.ppermute(value, axis, [(i, i ^ bit) for i in range(lax.axis_size(axis...  11.2 us
    ppermute x6, waiting for transfers between devices, swapped(): lax.ppermute(value, axis, [(i, i ^ bit) for i in range(lax.axis_size(axis...  8.16 us
    ppermute x4, starting transfers between devices, shifted(): lax.ppermute(value, axis, [(i, (i + step) % count) for i in range(count)])  6.51 us
    pallas_call x5, Pallas kernels, call(): pl.pallas_call(kernel, out_shape=[jax.ShapeDtypeStruct(shape, dtype) for...  6.01 us
    all_to_all x1, starting transfers between devices, on_device(): lax.all_to_all(message, 'box', split_axis=0, concat_axis=0, tiled=True)  5.91 us
    ppermute x4, waiting for transfers between devices, shifted(): lax.ppermute(value, axis, [(i, (i + step) % count) for i in range(count)])  2.37 us
  transfers between devices with their start and end apart: 11, of which 3 were waited for; matrix products, arithmetic and copies ran while one was open for 0% of the time, Pallas kernels for 5%

profile of v1, /device:TPU:0, one launch (start us, length us, event | category | flops | bytes accessed | tf_op | source)
XLA Modules:
  0.0 40.2 jit_solution(18330409148465849188)
XLA Ops:
  0.0 1.4 %shard_map.73 = (f32[64,128]{1,0:T(8,128)S(1)}, f32[64,384]{1,0:T(8,128)S(1)}, bf16[128,256]{1,0:T(8,128)(2,1)S(1)}, bf16[128,256]{1,0:T(8,128)(2,1)S(1)}) custom-call(f32[3,128]{1,0:T(4,128)} %points_in.1, s32[1,128]{1,0:T(1,128)} %bitcast.1, s32[1,32]{1,0:T(1,128)} %skeleton_in.3, f32[1,2,128,128]{3,2,1,0:T(8,128)} %inverse_in.3, f32[1,2,32,256]{3,2,1,0:T(8,128)} %top_in.1), custom_call_target="tpu_custom_call" | custom-call | tf_op jit(solution)/shard_map/pallas_call | solution.py:233
  1.4 4.1 %collective-permute-start.3 = (f32[64,384]{1,0:T(8,128)S(1)}, f32[64,384]{1,0:T(8,128)S(1)}, u32[]{:S(2)}, u32[]{:S(2)}) collective-permute-start(f32[64,384]{1,0:T(8,128)S(1)} %get-tuple-element.18.refs_0_), channel_id=1, source_target_pairs={{0,4},{1,5},{2,6},{3,7},{4,0},{5,1},{6,2},{7,3},{8,12},{9,13},{10,... | collective-permute-start | bytes 294920 | tf_op jit(solution)/shard_map/ppermute | solution.py:249
  5.5 1.6 %collective-permute-start.2 = (f32[64,384]{1,0:T(8,128)S(1)}, f32[64,384]{1,0:T(8,128)S(1)}, u32[]{:S(2)}, u32[]{:S(2)}) collective-permute-start(f32[64,384]{1,0:T(8,128)S(1)} %get-tuple-element.18.refs_0_), channel_id=1, source_target_pairs={{0,2},{1,3},{2,0},{3,1},{4,6},{5,7},{6,4},{7,5},{8,10},{9,11},{10,... | collective-permute-start | bytes 294920 | tf_op jit(solution)/shard_map/ppermute | solution.py:249
  7.1 1.5 %collective-permute-start = (f32[64,128]{1,0:T(8,128)S(1)}, f32[64,128]{1,0:T(8,128)S(1)}, u32[]{:S(2)}, u32[]{:S(2)}) collective-permute-start(f32[64,128]{1,0:T(8,128)S(1)} %get-tuple-element.17.u), channel_id=1, source_target_pairs={{0,1},{1,2},{2,3},{3,4},{4,5},{5,6},{6,7},{7,0},{8,9},{9,10},{10,1... | collective-permute-start | bytes 98312 | tf_op jit(solution)/shard_map/ppermute | solution.py:245
  8.6 3.2 %collective-permute-start.1 = (f32[64,128]{1,0:T(8,128)S(1)}, f32[64,128]{1,0:T(8,128)S(1)}, u32[]{:S(2)}, u32[]{:S(2)}) collective-permute-start(f32[64,128]{1,0:T(8,128)S(1)} %get-tuple-element.17.u), channel_id=1, source_target_pairs={{0,7},{1,0},{2,1},{3,2},{4,3},{5,4},{6,5},{7,6},{8,15},{9,8},{10,9... | collective-permute-start | bytes 98312 | tf_op jit(solution)/shard_map/ppermute | solution.py:245
  11.8 1.9 %shard_map.74 = (f32[128,320]{1,0:T(8,128)S(1)}, bf16[512,320]{1,0:T(8,128)(2,1)S(1)}, bf16[512,320]{1,0:T(8,128)(2,1)S(1)}) custom-call(bf16[128,256]{1,0:T(8,128)(2,1)S(1)} %get-tuple-element.14.high, bf16[128,256]{1,0:T(8,128)(2,1)S(1)} %get-tuple-element.15.low, s32[1,32]{1,0:T(1,128)} %skeleton_in.3, s32[1,8]{1,0:T(1,128)} %mask_in.1, ...), custom_call_target="tpu_custom_call" | custom-call | tf_op jit(solution)/shard_map/pallas_call | solution.py:233
  13.7 0.0 collective-permute-done.left
  13.7 0.0 collective-permute-done.1.right
  13.7 0.0 collective-permute-done.3.four.refs_1_
  13.7 0.0 collective-permute-done.2.two.refs_2_
  13.8 0.1 collective-permute-start.4
  13.8 1.7 %collective-permute-start.5 = (f32[3,64,128]{2,1,0:T(8,128)S(1)}, f32[3,64,128]{2,1,0:T(8,128)S(1)}, u32[]{:S(2)}, u32[]{:S(2)}) collective-permute-start(f32[3,64,128]{2,1,0:T(8,128)S(1)} %get-tuple-element.19.middle), channel_id=1, source_target_pairs={{0,24},{8,0},{16,8},{24,16},{1,25},{9,1},{17,9},{25,17},{2,26},{10... | collective-permute-start | bytes 294920 | tf_op jit(solution)/shard_map/ppermute | solution.py:245
  15.6 2.3 %collective-permute-done.4.up = f32[3,64,128]{2,1,0:T(8,128)S(1)} collective-permute-done((f32[3,64,128]{2,1,0:T(8,128)S(1)}, f32[3,64,128]{2,1,0:T(8,128)S(1)}, u32[]{:S(2)}, u32[]{:S(2)}) %collective-permute-start.4) | collective-permute-done | bytes 98336 | tf_op jit(solution)/shard_map/ppermute | solution.py:245
  17.9 0.1 collective-permute-done.5.down
  17.9 1.2 %shard_map.76 = f32[8,40,128]{2,1,0:T(8,128)} custom-call(f32[3,64,128]{2,1,0:T(8,128)S(1)} %collective-permute-done.4.up, f32[3,64,128]{2,1,0:T(8,128)S(1)} %get-tuple-element.19.middle, f32[3,64,128]{2,1,0:T(8,128)S(1)} %collective-permute-done.5.down, f32[128,320]{1,0:T(8,128)S(1)} %get-tuple-element.16.base, ...), custom_call_target="tpu_custom_call" | custom-call | tf_op jit(solution)/shard_map/pallas_call | solution.py:233
  19.1 5.9 %all-to-all-start = ((f32[8,40,128]{2,1,0:T(8,128)}), f32[8,40,128]{2,1,0:T(8,128)S(1)}, u32[]{:S(2)}, u32[]{:S(2)}) async-start(f32[8,40,128]{2,1,0:T(8,128)} %shard_map.76), calls=%async_computation | async-start | bytes 327680 | tf_op jit(solution)/shard_map/all_to_all | solution.py:304
  25.0 2.0 %collective-permute-start.7 = (f32[2,64,384]{2,1,0:T(8,128)S(1)}, f32[2,64,384]{2,1,0:T(8,128)S(1)}, u32[]{:S(2)}, u32[]{:S(2)}) collective-permute-start(f32[2,64,384]{2,1,0:T(8,128)S(1)} %get-tuple-element.22), channel_id=1, source_target_pairs={{0,1},{1,0},{2,3},{3,2},{4,5},{5,4},{6,7},{7,6},{8,9},{9,8},{10,11... | collective-permute-start | bytes 589832 | tf_op jit(solution)/shard_map/ppermute | solution.py:249
  27.0 0.0 collective-permute-start.6
  27.1 2.0 %collective-permute-start.8 = (f32[64,384]{1,0:T(8,128)S(1)}, f32[64,384]{1,0:T(8,128)S(1)}, u32[]{:S(2)}, u32[]{:S(2)}) collective-permute-start(f32[64,384]{1,0:T(8,128)S(1)} %collective-permute-done.3.four.refs_1_), channel_id=1, source_target_pairs={{0,2},{1,3},{2,0},{3,1},{4,6},{5,7},{6,4},{7,5},{8,10},{9,11},{10,... | collective-permute-start | bytes 294920 | tf_op jit(solution)/shard_map/ppermute | solution.py:249
  29.1 1.5 %collective-permute-start.9 = (f32[64,384]{1,0:T(8,128)S(1)}, f32[64,384]{1,0:T(8,128)S(1)}, u32[]{:S(2)}, u32[]{:S(2)}) collective-permute-start(f32[64,384]{1,0:T(8,128)S(1)} %collective-permute-done.3.four.refs_1_), channel_id=1, source_target_pairs={{0,3},{1,2},{2,1},{3,0},{4,7},{5,6},{6,5},{7,4},{8,11},{9,10},{10,... | collective-permute-start | bytes 294920 | tf_op jit(solution)/shard_map/ppermute | solution.py:249
  30.5 8.1 %collective-permute-done.6.refs_3_ = f32[64,384]{1,0:T(8,128)S(1)} collective-permute-done((f32[64,384]{1,0:T(8,128)S(1)}, f32[64,384]{1,0:T(8,128)S(1)}, u32[]{:S(2)}, u32[]{:S(2)}) %collective-permute-start.6) | collective-permute-done | bytes 98336 | tf_op jit(solution)/shard_map/ppermute | solution.py:249
  38.7 0.0 collective-permute-done.7.refs_4_
  38.7 0.0 all-to-all-done.message
  38.7 1.5 %shard_map.77 = f32[2,16,1024]{2,1,0:T(8,128)} custom-call(f32[8,40,128]{2,1,0:T(8,128)S(1)} %all-to-all-done.message, f32[64,384]{1,0:T(8,128)S(1)} %get-tuple-element.18.refs_0_, f32[64,384]{1,0:T(8,128)S(1)} %collective-permute-done.3.four.refs_1_, f32[64,384]{1,0:T(8,128)S(1)} %collective-permute-done.2.two.refs_2_, ...), custom_call_target="tpu_custom_call" | custom-call | tf_op jit(solution)/shard_map/pallas_call | solution.py:233
  (3 shorter events, 0.0 us)
Async XLA Ops:
  1.4 12.4 %collective-permute-start.3 = (f32[64,384]{1,0:T(8,128)S(1)}, f32[64,384]{1,0:T(8,128)S(1)}, u32[]{:S(2)}, u32[]{:S(2)}) collective-permute-start(f32[64,384]{1,0:T(8,128)S(1)} %get-tuple-element.18.refs_0_), channel_id=1, source_target_pairs={{0,4},{1,5},{2,6},{3,7},{4,0},{5,1},{6,2},{7,3},{8,12},{9,13},{10,... | collective-permute-start | bytes 294920 | tf_op jit(solution)/shard_map/ppermute | solution.py:249
  5.5 8.3 %collective-permute-start.2 = (f32[64,384]{1,0:T(8,128)S(1)}, f32[64,384]{1,0:T(8,128)S(1)}, u32[]{:S(2)}, u32[]{:S(2)}) collective-permute-start(f32[64,384]{1,0:T(8,128)S(1)} %get-tuple-element.18.refs_0_), channel_id=1, source_target_pairs={{0,2},{1,3},{2,0},{3,1},{4,6},{5,7},{6,4},{7,5},{8,10},{9,11},{10,... | collective-permute-start | bytes 294920 | tf_op jit(solution)/shard_map/ppermute | solution.py:249
  7.1 6.7 %collective-permute-start = (f32[64,128]{1,0:T(8,128)S(1)}, f32[64,128]{1,0:T(8,128)S(1)}, u32[]{:S(2)}, u32[]{:S(2)}) collective-permute-start(f32[64,128]{1,0:T(8,128)S(1)} %get-tuple-element.17.u), channel_id=1, source_target_pairs={{0,1},{1,2},{2,3},{3,4},{4,5},{5,6},{6,7},{7,0},{8,9},{9,10},{10,1... | collective-permute-start | bytes 98312 | tf_op jit(solution)/shard_map/ppermute | solution.py:245
  8.6 5.1 %collective-permute-start.1 = (f32[64,128]{1,0:T(8,128)S(1)}, f32[64,128]{1,0:T(8,128)S(1)}, u32[]{:S(2)}, u32[]{:S(2)}) collective-permute-start(f32[64,128]{1,0:T(8,128)S(1)} %get-tuple-element.17.u), channel_id=1, source_target_pairs={{0,7},{1,0},{2,1},{3,2},{4,3},{5,4},{6,5},{7,6},{8,15},{9,8},{10,9... | collective-permute-start | bytes 98312 | tf_op jit(solution)/shard_map/ppermute | solution.py:245
  13.8 4.1 %collective-permute-start.4 = (f32[3,64,128]{2,1,0:T(8,128)S(1)}, f32[3,64,128]{2,1,0:T(8,128)S(1)}, u32[]{:S(2)}, u32[]{:S(2)}) collective-permute-start(f32[3,64,128]{2,1,0:T(8,128)S(1)} %get-tuple-element.19.middle), channel_id=1, source_target_pairs={{0,8},{8,16},{16,24},{24,0},{1,9},{9,17},{17,25},{25,1},{2,10},{10... | collective-permute-start | bytes 294920 | tf_op jit(solution)/shard_map/ppermute | solution.py:245
  13.8 4.1 %collective-permute-start.5 = (f32[3,64,128]{2,1,0:T(8,128)S(1)}, f32[3,64,128]{2,1,0:T(8,128)S(1)}, u32[]{:S(2)}, u32[]{:S(2)}) collective-permute-start(f32[3,64,128]{2,1,0:T(8,128)S(1)} %get-tuple-element.19.middle), channel_id=1, source_target_pairs={{0,24},{8,0},{16,8},{24,16},{1,25},{9,1},{17,9},{25,17},{2,26},{10... | collective-permute-start | bytes 294920 | tf_op jit(solution)/shard_map/ppermute | solution.py:245
  19.1 19.6 %all-to-all-start = ((f32[8,40,128]{2,1,0:T(8,128)}), f32[8,40,128]{2,1,0:T(8,128)S(1)}, u32[]{:S(2)}, u32[]{:S(2)}) async-start(f32[8,40,128]{2,1,0:T(8,128)} %shard_map.76), calls=%async_computation | async-start | bytes 327680 | tf_op jit(solution)/shard_map/all_to_all | solution.py:304
  25.0 13.7 %collective-permute-start.7 = (f32[2,64,384]{2,1,0:T(8,128)S(1)}, f32[2,64,384]{2,1,0:T(8,128)S(1)}, u32[]{:S(2)}, u32[]{:S(2)}) collective-permute-start(f32[2,64,384]{2,1,0:T(8,128)S(1)} %get-tuple-element.22), channel_id=1, source_target_pairs={{0,1},{1,0},{2,3},{3,2},{4,5},{5,4},{6,7},{7,6},{8,9},{9,8},{10,11... | collective-permute-start | bytes 589832 | tf_op jit(solution)/shard_map/ppermute | solution.py:249
  27.0 11.6 %collective-permute-start.6 = (f32[64,384]{1,0:T(8,128)S(1)}, f32[64,384]{1,0:T(8,128)S(1)}, u32[]{:S(2)}, u32[]{:S(2)}) collective-permute-start(f32[64,384]{1,0:T(8,128)S(1)} %get-tuple-element.18.refs_0_), channel_id=1, source_target_pairs={{0,1},{1,0},{2,3},{3,2},{4,5},{5,4},{6,7},{7,6},{8,9},{9,8},{10,11... | collective-permute-start | bytes 294920 | tf_op jit(solution)/shard_map/ppermute | solution.py:249
  27.1 11.6 %collective-permute-start.8 = (f32[64,384]{1,0:T(8,128)S(1)}, f32[64,384]{1,0:T(8,128)S(1)}, u32[]{:S(2)}, u32[]{:S(2)}) collective-permute-start(f32[64,384]{1,0:T(8,128)S(1)} %collective-permute-done.3.four.refs_1_), channel_id=1, source_target_pairs={{0,2},{1,3},{2,0},{3,1},{4,6},{5,7},{6,4},{7,5},{8,10},{9,11},{10,... | collective-permute-start | bytes 294920 | tf_op jit(solution)/shard_map/ppermute | solution.py:249
  29.1 9.6 %collective-permute-start.9 = (f32[64,384]{1,0:T(8,128)S(1)}, f32[64,384]{1,0:T(8,128)S(1)}, u32[]{:S(2)}, u32[]{:S(2)}) collective-permute-start(f32[64,384]{1,0:T(8,128)S(1)} %collective-permute-done.3.four.refs_1_), channel_id=1, source_target_pairs={{0,3},{1,2},{2,1},{3,0},{4,7},{5,6},{6,5},{7,4},{8,11},{9,10},{10,... | collective-permute-start | bytes 294920 | tf_op jit(solution)/shard_map/ppermute | solution.py:249
